TPU v7x, 256 devices: a whole 4x4x8 slice. The times are simulated.
256 devices in a mesh: row: 32 (over z, x), col: 8 (over y, core).
Axes of the slice: x: 4, y: 4, z: 8, core: 2. Of those that a mesh axis runs over, the one named last changes fastest.
Arguments:
- activations: bfloat16 [2048, 16384], P('col', 'row'), may hold values from -6 to 6
- out_grads: bfloat16 [2048, 26624], P('row', 'col'), may hold values from -0.125 to 0.125
- weights: bfloat16 [16384, 26624], P('row', 'col'), may hold values from -0.119628906 to 0.119628906
- projector: bfloat16 [256, 16384], P(None, 'row')
- first_moment: float32 [256, 26624], P('row', 'col'), may hold values from -4 to 4
- second_moment: float32 [256, 26624], P('row', 'col'), may hold values from 1e-06 to 0.03
Outputs:
- new_weights: bfloat16 [16384, 26624], P('row', 'col')
- new_first: float32 [256, 26624], P('row', 'col')
- new_second: float32 [256, 26624], P('row', 'col')
All inputs are finite; a program needn't handle non-finite values.
Results may differ from a plain program's by a relative error of at most 0.01005.
Values may be sent and summed in bfloat16 or wider, within the bound.
A program may use at most 64 MiB of HBM per device.

v0:
```python
import jax
import jax.numpy as jnp
from jax import lax
from jax.sharding import PartitionSpec as P

STEP = 10


def shards(activations, out_grads, weights, projector, first_moment, second_moment):
    gathered = lax.all_gather(activations, "col", axis=0, tiled=True)
    own_rows = first_moment.shape[0]
    grad_full = lax.dot_general(
        gathered,
        lax.all_gather(out_grads, "row", axis=0, tiled=True),
        (((0,), (0,)), ((), ())),
        preferred_element_type=jnp.float32,
    )
    grad = grad_full.astype(jnp.bfloat16)
    partial_proj = jnp.dot(
        projector.astype(jnp.float32), grad_full, precision=lax.Precision.HIGHEST
    )
    summed = lax.psum(partial_proj, "row")
    proj = lax.dynamic_slice_in_dim(summed, lax.axis_index("row") * own_rows, own_rows, 0)
    first = 0.9 * first_moment + 0.1 * proj
    second = 0.999 * second_moment + 0.001 * proj * proj
    normed = first / (1.0 - 0.9**STEP) / (jnp.sqrt(second / (1.0 - 0.999**STEP)) + 1e-08)
    normed_sq, proj_sq = lax.psum(
        (jnp.sum(normed * normed, axis=0), jnp.sum(proj * proj, axis=0)), "row"
    )
    scale = jnp.sqrt(normed_sq) / jnp.sqrt(proj_sq + 1e-06)
    new_weights = (
        weights.astype(jnp.float32) - 0.01 * scale[None, :] * grad.astype(jnp.float32)
    ).astype(jnp.bfloat16)
    return (new_weights, first, second)


def solution(mesh):
    return jax.shard_map(
        shards,
        mesh=mesh,
        in_specs=(
            P("col", "row"),
            P("row", "col"),
            P("row", "col"),
            P(None, "row"),
            P("row", "col"),
            P("row", "col"),
        ),
        out_specs=(P("row", "col"), P("row", "col"), P("row", "col")),
        check_vma=False,
    )
```

profile of v0, /device:TPU:8, one launch (start us, length us, event | category | flops | bytes accessed | tf_op | source)
XLA Modules:
  0.0 499.9 jit_solution(16654426909176899853)
XLA Ops:
  7.2 0.0 copy-start
  7.2 0.0 all-gather.3.cloned.1.call-start
  7.2 0.7 all-gather.3.cloned.1.call-update
  7.9 0.0 all-gather.5.cloned.1.call-start
  8.0 0.7 all-gather.5.cloned.1.call-update
  8.7 0.0 all-reduce.3.cloned.1.call-start
  8.7 30.9 %all-gather.3.cloned.1.call-done = bf16[2048,512]{1,0:T(8,128)(2,1)} async-done(((bf16[256,512]{1,0:T(8,128)(2,1)}), bf16[2048,512]{1,0:T(8,128)(2,1)}) %all-gather.3.cloned.1.call-update) | async-done | bytes 2097168 | tf_op jit(solution)/shard_map/all_gather | solution.py:10
  39.6 128.4 %all-gather.5.cloned.1.call-done = bf16[2048,3328]{1,0:T(8,128)(2,1)} async-done(((bf16[64,3328]{1,0:T(8,128)(2,1)}), bf16[2048,3328]{1,0:T(8,128)(2,1)}) %all-gather.5.cloned.1.call-update) | async-done | bytes 13631504 | tf_op jit(solution)/shard_map/all_gather | solution.py:14
  168.0 11.9 %fusion.2 = f32[512,3328]{1,0:T(8,128)S(1)} fusion(bf16[2048,512]{1,0:T(8,128)(2,1)} %all-gather.3.cloned.1.call-done, bf16[2048,3328]{1,0:T(8,128)(2,1)} %all-gather.5.cloned.1.call-done), kind=kOutput, calls=%fused_computation.8 | convolution fusion | flops 6979321856 | bytes 22544384 | tf_op jit(solution)/shard_map/dot_general | solution.py:12
  179.9 0.0 copy-start.1
  179.9 2.8 copy-done.1
  182.7 0.0 copy-done
  182.7 0.0 copy-start.2
  182.7 0.0 copy-start.3
  182.7 5.4 %convolution_bitcast_fusion = f32[256,3328]{1,0:T(8,128)} fusion(f32[512,3328]{1,0:T(8,128)S(1)} %fusion.2, bf16[256,512]{1,0:T(8,128)(2,1)S(1)} %copy-done), kind=kOutput, calls=%fused_computation.1 | convolution fusion | flops 5234491392 | bytes 10485760 | tf_op jit(solution)/shard_map/dot_general | solution.py:19
  188.1 0.0 all-reduce.3.cloned.1.call-update
  188.1 157.1 %all-reduce.3.cloned.1.call-done = f32[256,3328]{1,0:T(8,128)} async-done(((f32[256,3328]{1,0:T(8,128)}), f32[256,3328]{1,0:T(8,128)}) %all-reduce.3.cloned.1.call-update) | async-done | bytes 3407888 | tf_op jit(solution)/shard_map/psum | solution.py:22
  345.2 0.0 copy-done.2
  345.2 0.0 copy-done.3
  345.2 1.6 multiply_reduce_fusion.1
  346.9 140.0 %all-reduce = (f32[3328]{0:T(1024)S(1)}, f32[3328]{0:T(1024)S(1)}) all-reduce(f32[3328]{0:T(1024)S(1)} %get-tuple-element.11, f32[3328]{0:T(1024)S(1)} %get-tuple-element.8), channel_id=1, replica_groups=mesh['row'=32,'col'=8] {'row'}, use_global_device_ids=true, to_apply=%region_4.0 | all-reduce | flops 6656 | bytes 53248 | tf_op jit(solution)/shard_map/psum | solution.py:27
  486.9 6.5 %subtract_convert_fusion = bf16[512,3328]{1,0:T(8,128)(2,1)} fusion(bf16[512,3328]{1,0:T(8,128)(2,1)} %param.8, f32[512,3328]{1,0:T(8,128)} %copy-done.1, f32[3328]{0:T(1024)S(1)} %multiply_multiply_fusion.1), kind=kLoop, calls=%fused_computation | loop fusion | flops 10223616 | bytes 13644800 | tf_op jit(solution)/shard_map/convert_element_type | solution.py:33
  (1 shorter events, 0.0 us)
Async XLA Ops:
  7.2 175.5 %copy-start = (bf16[256,512]{1,0:T(8,128)(2,1)S(1)}, bf16[256,512]{1,0:T(8,128)(2,1)}, u32[]{:S(2)}) copy-start(bf16[256,512]{1,0:T(8,128)(2,1)} %param.9) | copy-start | bytes 786436
  7.2 32.4 %all-gather.3.cloned.1.call-start = ((), (), s32[]{:S(2)}) async-start(), calls=%async_computation | async-start | bytes 2359296 | tf_op jit(solution)/shard_map/all_gather | solution.py:10
  7.9 160.1 %all-gather.5.cloned.1.call-start = ((), (), s32[]{:S(2)}) async-start(), calls=%async_computation.1 | async-start | bytes 14057472 | tf_op jit(solution)/shard_map/all_gather | solution.py:14
  8.7 336.6 %all-reduce.3.cloned.1.call-start = ((), (), s32[]{:S(2)}) async-start(), calls=%async_computation.2 | async-start | bytes 6815744 | tf_op jit(solution)/shard_map/psum | solution.py:22
  179.9 2.8 copy-start.1
  182.7 162.5 %copy-start.2 = (f32[8,3328]{1,0:T(8,128)S(1)}, f32[8,3328]{1,0:T(8,128)}, u32[]{:S(2)}) copy-start(f32[8,3328]{1,0:T(8,128)} %param.10) | copy-start | bytes 319492
  182.7 162.5 %copy-start.3 = (f32[8,3328]{1,0:T(8,128)S(1)}, f32[8,3328]{1,0:T(8,128)}, u32[]{:S(2)}) copy-start(f32[8,3328]{1,0:T(8,128)} %param.11) | copy-start | bytes 319492
Sparse Core Ops, SparseCore 0:
  9.9 29.6 all-gather.2
  42.2 125.7 all-gather.4
  188.2 156.9 all-reduce.2
where the time goes:
time: 500 us
  waiting for transfers between devices  318 us (64%)
  blocking collectives  140 us (28%)
  matrix products  17.3 us (3%)
  between operations  13.8 us (3%)
  other arithmetic  8.17 us (2%)
    psum x1, waiting for transfers between devices, shards(): summed = lax.psum(partial_proj, 'row')  157 us
    psum x1, blocking collectives, shards(): lax.psum((jnp.sum(normed * normed, axis=0), jnp.sum(proj * proj, axis=0))...  140 us
    all_gather x1, waiting for transfers between devices, shards(): lax.all_gather(out_grads, 'row', axis=0, tiled=True)  128 us
    all_gather x1, waiting for transfers between devices, shards(): gathered = lax.all_gather(activations, 'col', axis=0, tiled=True)  30.9 us
    dot_general x1, matrix products, shards(): lax.dot_general(gathered, lax.all_gather(out_grads, 'row', axis=0, tiled=...  11.9 us
  transfers between devices with their start and end apart: 3, of which 3 were waited for; matrix products, arithmetic and copies ran while one was open for 0% of the time, Pallas kernels for 0%

commit v1 on v0

v1 whole, which is shorter than its diff:
```python
import jax
import jax.numpy as jnp
from jax import lax
from jax.experimental import pallas as pl
from jax.experimental.pallas import tpu as pltpu
from jax.sharding import PartitionSpec as P

STEP = 10
MESH = pl.DeviceIdType.MESH
BF = jnp.bfloat16
F32 = jnp.float32

NZ, NX, NY = 8, 4, 4
NCH = 13
LAG = 2
FIRST_C = 5 + LAG
TICKS = NCH + FIRST_C + 3


def kernel(
    act, og, w, pj, m1, m2, ow, o1, o2,
    avm, ogv, pv, wv, m1v, m2v, at, av1, g, gs, gr, go, ps, pr, po,
    s1s, s1r, s2s, s2r, qpart, qx, qs, qz, qsend,
    loc, r_p, r_b, r_z, r_m, r_g, r_pr, r_s1, r_s2, r_a, r_h, r_q, snd, outs,
):
    row, col = lax.axis_index("row"), lax.axis_index("col")
    z, x = row // 4, lax.rem(row, 4)
    y, core = col // 2, lax.rem(col, 2)
    pair_x = x + 1 - 2 * lax.rem(x, 2)
    mate_x = 3 - x
    cls = lax.rem((x + 1) // 2, 2)

    def at_z(d):
        return (lax.rem(z + d, NZ) * 4 + x, col)

    def at_x(d):
        return (z * 4 + lax.rem(x + d, NX), col)

    def at_y(d):
        return (row, lax.rem(y + d, NY) * 2 + core)

    def at_col(d):
        return (row, lax.rem(col + d, 8))

    up, down = at_z(1), at_z(NZ - 1)
    pair, mate = (z * 4 + pair_x, col), (z * 4 + mate_x, col)
    y_up, y_down = at_y(1), at_y(NY - 1)
    sibling = (row, y * 2 + 1 - core)

    def send(src, dst, ssem, rsem, target):
        pltpu.make_async_remote_copy(
            src_ref=src, dst_ref=dst, send_sem=ssem, recv_sem=rsem, device_id=target, device_id_type=MESH
        ).start()

    def wait(ref, sem):
        pltpu.make_async_copy(ref, ref, sem).wait()

    barrier = pltpu.get_barrier_semaphore()
    partners = [at_z(d) for d in range(1, NZ)] + [at_x(d) for d in range(1, NX)] + [at_col(d) for d in range(1, 8)]
    for partner in partners:
        pl.semaphore_signal(barrier, inc=1, device_id=partner, device_id_type=MESH)

    loads = [(act, avm), (og, ogv), (pj, pv), (w, wv), (m1, m1v), (m2, m2v)]
    for k, (src, dst) in enumerate(loads):
        pltpu.make_async_copy(src, dst, loc.at[k]).start()

    own_lanes = pl.ds(pl.multiple_of(col * 256, 256), 256)
    PAIR, OWN = 0, 528
    pltpu.make_async_copy(act, avm, loc.at[0]).wait()

    def turned(xx):
        parts = []
        for j in range(4):
            lo = lax.rem(xx, 2)
            hi = xx // 2
            lo = 1 - lo if j % 2 else lo
            hi = 1 - hi if j // 2 else hi
            parts.append(avm[pl.ds(pl.multiple_of((hi * 2 + lo) * 64, 64), 64), :])
        return jnp.concatenate(parts, axis=0).T

    av1[...] = turned(pair_x)
    at[pl.ds(OWN, 512), own_lanes] = turned(x)
    pltpu.make_async_copy(og, ogv, loc.at[1]).wait()
    pl.semaphore_wait(barrier, len(partners))

    def block(zz, start, size):
        return pl.ds(pl.multiple_of(zz * 256 + start, 32), size)

    def zrel(d):
        return lax.rem(z + d, NZ)

    def columns(which, c):
        return pl.ds(pl.multiple_of((which * NCH + c) * 128, 128), 128)

    S_Z, S_M, S_P, S_G, S_PR, S_S1, S_S2, S_AP, S_AO, S_H, S_QX, S_QZ, S_QC, S_QP = range(14)

    def p_stage(c):
        send(ogv.at[:, columns(1 - cls, c)], g.at[c, block(z, 64, 64)], snd.at[S_P], r_p.at[c], pair)

    def b1_stage(c):
        wait(g.at[c, block(z, 64, 64)], r_p.at[c])
        send(g.at[c, block(z, 64, 64)], g.at[c, block(z, 128, 64)], snd.at[S_M], r_b.at[c], mate)

    def b2_stage(c):
        wait(g.at[c, block(z, 128, 64)], r_b.at[c])
        part = g.at[c, block(z, 64, 128)]
        send(part, part, snd.at[S_Z], r_z.at[c, 0], up)
        send(part, part, snd.at[S_Z], r_z.at[c, 1], down)

    def to_mate(c, zz):
        send(g.at[c, block(zz, 0, 64)], g.at[c, block(zz, 192, 64)], snd.at[S_M], r_m.at[c], mate)

    def e0_stage(c):
        g[c, block(z, 0, 64), :] = ogv[:, columns(cls, c)]
        part = g.at[c, block(z, 0, 64)]
        send(part, part, snd.at[S_Z], r_z.at[c, 0], up)
        send(part, part, snd.at[S_Z], r_z.at[c, 1], down)
        to_mate(c, z)

    def z_stage(c, hop):
        lower, upper = zrel(NZ - hop), zrel(hop)
        if hop == 4:
            wait(g.at[c, block(lower, 0, 192)], r_z.at[c, 6])
            to_mate(c, lower)
            return
        a, b = (0, 192) if hop < 3 else (0, 96)
        wait(g.at[c, block(lower, 0, 192)], r_z.at[c, 2 * hop - 2])
        part = g.at[c, block(lower, a, b)]
        send(part, part, snd.at[S_Z], r_z.at[c, 2 * hop if hop < 3 else 6], up)
        a, b = (0, 192) if hop < 3 else (96, 96)
        wait(g.at[c, block(upper, 0, 192)], r_z.at[c, 2 * hop - 1])
        part = g.at[c, block(upper, a, b)]
        send(part, part, snd.at[S_Z], r_z.at[c, 2 * hop + 1 if hop < 3 else 6], down)
        to_mate(c, lower)
        to_mate(c, upper)

    def a_ref(panel, yy, start, size):
        lanes = pl.ds(pl.multiple_of((yy * 2 + core) * 256, 256), 256)
        return at.at[pl.ds((PAIR, OWN)[panel] + start, size), lanes]

    def a_send(panel, yy, start, size, sem, target):
        part = a_ref(panel, yy, start, size)
        send(part, part, snd.at[S_AP + panel], r_a.at[panel, sem], target)

    def a_start(panel, h):
        if panel == 0:
            wait(a_ref(0, y, 256 * h, 256), r_h.at[h])
        a_send(panel, y, 256 * h, 256, h, y_up)
        a_send(panel, y, 256 * h, 256, 2 + h, y_down)
        a_send(panel, y, 256 * h, 256, 6, sibling)

    y_lower, y_upper, y_far = lax.rem(y + 3, NY), lax.rem(y + 1, NY), lax.rem(y + 2, NY)

    def a_arrive(panel, h):
        wait(a_ref(panel, y_lower, 256 * h, 256), r_a.at[panel, h])
        if h == 0:
            a_send(panel, y_lower, 0, 256, 4, y_up)
        wait(a_ref(panel, y_upper, 256 * h, 256), r_a.at[panel, 2 + h])
        if h == 1:
            a_send(panel, y_upper, 256, 256, 5, y_down)
        a_send(panel, y_lower, 256 * h, 256, 6, sibling)
        a_send(panel, y_upper, 256 * h, 256, 6, sibling)

    def a_far(panel):
        wait(a_ref(panel, y_far, 0, 256), r_a.at[panel, 4])
        wait(a_ref(panel, y_far, 256, 256), r_a.at[panel, 5])
        a_send(panel, y_far, 0, 512, 6, sibling)

    def a_done(panel):
        wait(at.at[pl.ds((PAIR, OWN)[panel], 512), pl.ds(0, 1024)], r_a.at[panel, 6])

    def q_part():
        pltpu.make_async_copy(pj, pv, loc.at[2]).wait()
        q = lax.dot_general(pv[...], avm[...], (((1,), (1,)), ((), ())), preferred_element_type=F32)
        for xx in range(NX):
            for zz in range(NZ):
                start = 8 * (4 * zz + xx)
                qpart[xx, zz] = q[start : start + 8]
        for d in range(1, NX):
            send(qpart.at[lax.rem(x + d, NX)], qx.at[d - 1], snd.at[S_QX], r_q.at[0], at_x(d))

    def q_over_x():
        wait(qx, r_q.at[0])
        qs[...] = qpart[x] + qx[0] + qx[1] + qx[2]
        for d in range(1, NZ):
            send(qs.at[zrel(d)], qz.at[d - 1], snd.at[S_QZ], r_q.at[1], at_z(d))

    q_rows = at.at[pl.ds(OWN + 512, 16), own_lanes]

    def q_over_z():
        wait(qz, r_q.at[1])
        q = qs[z]
        for d in range(NZ - 1):
            q = q + qz[d]
        left, right = q[:, :128], q[:, 128:]
        odd = lax.rem(x, 2) == 1
        left = jnp.where(odd, pltpu.roll(left, 64, 1), left)
        right = jnp.where(odd, pltpu.roll(right, 64, 1), right)
        late = x >= 2
        q = jnp.concatenate([jnp.where(late, right, left), jnp.where(late, left, right)], axis=1)
        high = q.astype(BF).astype(F32)
        at[pl.ds(OWN + 512, 16), own_lanes] = jnp.concatenate([high, q - high], axis=0).astype(BF)
        for d in range(1, 8):
            send(q_rows, q_rows, snd.at[S_QC], r_q.at[2], at_col(d))

    def q_to_pair():
        wait(at.at[pl.ds(OWN + 512, 16), pl.ds(0, 1792)], r_q.at[2])
        for k in range(16):
            part = at[pl.ds(OWN + 512, 16), pl.ds(128 * k, 128)].astype(F32)
            qsend[:, pl.ds(128 * k, 128)] = pltpu.roll(part, 64, 1).astype(BF)
        send(qsend, at.at[pl.ds(PAIR + 512, 16), :], snd.at[S_QP], r_q.at[3], pair)

    def c_stage(c):
        wait(g.at[c, pl.ds(0, 512)], r_m.at[c])
        total = jnp.dot(at[pl.ds(PAIR, 528), :], g[c], preferred_element_type=F32)
        gs[c] = total[:512].astype(BF)
        ps[c] = total[512:520] + total[520:528]
        send(ps.at[c], pr.at[c], snd.at[S_PR], r_pr.at[c], pair)
        send(gs.at[c], gr.at[c], snd.at[S_G], r_g.at[c], pair)
        total = jnp.dot(at[pl.ds(OWN, 528), :], g[c], preferred_element_type=F32)
        go[c] = total[:512].astype(BF)
        po[c] = total[512:520] + total[520:528]

    def moments(proj, cols):
        first = 0.9 * m1v[:, cols] + 0.1 * proj
        second = 0.999 * m2v[:, cols] + 0.001 * proj * proj
        m1v[:, cols] = first
        m2v[:, cols] = second
        normed = first / (1.0 - 0.9**STEP) / (jnp.sqrt(second / (1.0 - 0.999**STEP)) + 1e-08)
        return jnp.sum(normed * normed, axis=0, keepdims=True), jnp.sum(proj * proj, axis=0, keepdims=True)

    def s1_stage(c):
        wait(pr.at[c], r_pr.at[c])
        n_own, p_own = moments(po[c], columns(cls, c))
        n_oth, p_oth = moments(pr[c], columns(1 - cls, c))
        first = cls == 0
        s1s[c, 0:1] = jnp.where(first, n_own, n_oth)
        s1s[c, 1:2] = jnp.where(first, p_own, p_oth)
        s1s[c, 2:3] = jnp.where(first, n_oth, n_own)
        s1s[c, 3:4] = jnp.where(first, p_oth, p_own)
        s1s[c, 4:8] = jnp.zeros((4, 128), F32)
        for d in range(1, NX):
            send(s1s.at[c], s1r.at[c, d - 1], snd.at[S_S1], r_s1.at[c], at_x(d))

    def s2_stage(c):
        wait(s1r.at[c], r_s1.at[c])
        s2s[c] = s1s[c] + s1r[c, 0] + s1r[c, 1] + s1r[c, 2]
        for d in range(1, NZ):
            send(s2s.at[c], s2r.at[c, d - 1], snd.at[S_S2], r_s2.at[c], at_z(d))

    def update(cols, grad, scale):
        wv[:, cols] = (wv[:, cols].astype(F32) - 0.01 * scale * grad.astype(F32)).astype(BF)
        pltpu.make_async_copy(wv.at[:, cols], ow.at[:, cols], outs.at[0]).start()

    def s3_stage(c):
        wait(s2r.at[c], r_s2.at[c])
        sums = s2s[c]
        for d in range(NZ - 1):
            sums = sums + s2r[c, d]
        scale_a = jnp.sqrt(sums[0:1]) / jnp.sqrt(sums[1:2] + 1e-06)
        scale_b = jnp.sqrt(sums[2:3]) / jnp.sqrt(sums[3:4] + 1e-06)
        first = cls == 0
        update(columns(cls, c), go[c], jnp.where(first, scale_a, scale_b))
        wait(gr.at[c], r_g.at[c])
        update(columns(1 - cls, c), gr[c], jnp.where(first, scale_b, scale_a))

    for c in range(2):
        p_stage(c)
    e0_stage(0)
    for h in range(2):
        send(
            av1.at[pl.ds(256 * h, 256)], at.at[pl.ds(PAIR + 256 * h, 256), own_lanes],
            snd.at[S_H], r_h.at[h], pair,
        )
    a_start(1, 0)
    q_part()
    b1_stage(0)

    def once(i, ticks, f):
        pl.when(i == ticks)(f)

    def stage(c, f):
        pl.when(jnp.logical_and(c >= 0, c < NCH))(lambda: f(c))

    @pl.loop(0, TICKS)
    def _(i):
        for hop in (4, 3, 2, 1):
            stage(i - hop, lambda c, hop=hop: z_stage(c, hop))
        stage(i, b2_stage)
        stage(i + 1, e0_stage)
        stage(i + 1, b1_stage)
        stage(i + 2, p_stage)

        @pl.when(i == 1)
        def _():
            a_start(0, 0)
            q_over_x()

        @pl.when(i == 2)
        def _():
            a_start(0, 1)
            a_start(1, 1)

        @pl.when(i == 3)
        def _():
            a_arrive(1, 0)
            q_over_z()

        @pl.when(i == 4)
        def _():
            a_arrive(0, 0)
            a_arrive(0, 1)
            q_to_pair()

        @pl.when(i == 5)
        def _():
            a_arrive(1, 1)
            a_far(0)

        @pl.when(i == 6)
        def _():
            a_far(1)
            pltpu.make_async_copy(m1, m1v, loc.at[4]).wait()
            pltpu.make_async_copy(m2, m2v, loc.at[5]).wait()
            pltpu.make_async_copy(w, wv, loc.at[3]).wait()

        @pl.when(i == FIRST_C)
        def _():
            a_done(0)
            a_done(1)
            wait(qsend, r_q.at[3])

        stage(i - FIRST_C, c_stage)
        stage(i - FIRST_C - 3, s3_stage)
        stage(i - FIRST_C - 2, s2_stage)
        stage(i - FIRST_C - 1, s1_stage)

        @pl.when(i == FIRST_C + NCH)
        def _():
            pltpu.make_async_copy(m1v, o1, outs.at[1]).start()
            pltpu.make_async_copy(m2v, o2, outs.at[2]).start()

    wait(g.at[:, pl.ds(0, 1344)], snd.at[S_Z])
    wait(g.at[:, pl.ds(0, 576)], snd.at[S_M])
    wait(g.at[:, pl.ds(0, 64)], snd.at[S_P])
    wait(gs, snd.at[S_G])
    wait(ps, snd.at[S_PR])
    wait(s1r, snd.at[S_S1])
    wait(s2r, snd.at[S_S2])
    wait(at.at[pl.ds(0, 512), pl.ds(0, 1792)], snd.at[S_AP])
    wait(at.at[pl.ds(0, 512), pl.ds(0, 1792)], snd.at[S_AO])
    wait(av1, snd.at[S_H])
    wait(qx, snd.at[S_QX])
    wait(qz, snd.at[S_QZ])
    wait(at.at[pl.ds(0, 16), pl.ds(0, 1792)], snd.at[S_QC])
    wait(qsend, snd.at[S_QP])
    wait(m1v, outs.at[1])
    wait(m2v, outs.at[2])
    wait(wv, outs.at[0])


def shards(activations, out_grads, weights, projector, first_moment, second_moment):
    vm, dma = pltpu.VMEM, pltpu.SemaphoreType.DMA
    return pl.pallas_call(
        kernel,
        out_shape=(
            jax.ShapeDtypeStruct((512, 3328), BF),
            jax.ShapeDtypeStruct((8, 3328), F32),
            jax.ShapeDtypeStruct((8, 3328), F32),
        ),
        in_specs=[pl.BlockSpec(memory_space=pl.ANY)] * 6,
        out_specs=(pl.BlockSpec(memory_space=pl.ANY),) * 3,
        scratch_shapes=[
            vm((256, 512), BF),
            vm((64, 3328), BF),
            vm((256, 512), BF),
            vm((512, 3328), BF),
            vm((8, 3328), F32),
            vm((8, 3328), F32),
            vm((1056, 2048), BF),
            vm((512, 256), BF),
            vm((NCH, 2048, 128), BF),
            vm((NCH, 512, 128), BF),
            vm((NCH, 512, 128), BF),
            vm((NCH, 512, 128), BF),
            vm((NCH, 8, 128), F32),
            vm((NCH, 8, 128), F32),
            vm((NCH, 8, 128), F32),
            vm((NCH, 8, 128), F32),
            vm((NCH, 3, 8, 128), F32),
            vm((NCH, 8, 128), F32),
            vm((NCH, 7, 8, 128), F32),
            vm((4, 8, 8, 256), F32),
            vm((3, 8, 8, 256), F32),
            vm((8, 8, 256), F32),
            vm((7, 8, 256), F32),
            vm((16, 2048), BF),
            dma((6,)),
            dma((NCH,)),
            dma((NCH,)),
            dma((NCH, 7)),
            dma((NCH,)),
            dma((NCH,)),
            dma((NCH,)),
            dma((NCH,)),
            dma((NCH,)),
            dma((2, 7)),
            dma((2,)),
            dma((4,)),
            dma((14,)),
            dma((3,)),
        ],
        compiler_params=pltpu.CompilerParams(
            collective_id=0, has_side_effects=True, vmem_limit_bytes=48 * 1024 * 1024
        ),
    )(activations, out_grads, weights, projector, first_moment, second_moment)


def solution(mesh):
    return jax.shard_map(
        shards,
        mesh=mesh,
        in_specs=(
            P("col", "row"),
            P("row", "col"),
            P("row", "col"),
            P(None, "row"),
            P("row", "col"),
            P("row", "col"),
        ),
        out_specs=(P("row", "col"), P("row", "col"), P("row", "col")),
        check_vma=False,
    )
```

time: 500 us -> 133 us (0.27)
  the two profiles are of different devices: /device:TPU:8 before, /device:TPU:10 now
where the time goes in v1:
time: 133 us
  Pallas kernels  125 us (94%)
  local copies, waits for them, and re-layouts  7.73 us (6%)
    pallas_call x1, Pallas kernels, shards(): pl.pallas_call(kernel, out_shape=(jax.ShapeDtypeStruct((512, 3328), BF),...  125 us
    unnamed x13, local copies, waits for them, and re-layouts  7.73 us

profile of v1, /device:TPU:10, one launch (start us, length us, event | category | flops | bytes accessed | tf_op | source)
XLA Modules:
  0.0 133.2 jit_solution(11922915896098190343)
XLA Ops:
  0.6 0.0 copy-start
  0.6 1.0 copy-done
  1.6 0.0 copy-start.1
  1.6 0.9 copy-done.1
  2.6 0.0 copy-start.2
  2.6 0.9 copy-done.2
  3.5 0.0 copy-start.3
  3.5 0.9 copy-done.3
  4.4 0.0 copy-start.4
  4.4 0.9 copy-done.4
  5.3 124.9 %shard_map.85 = (bf16[512,3328]{1,0:T(8,128)(2,1)S(1)}, f32[8,3328]{1,0:T(8,128)S(1)}, f32[8,3328]{1,0:T(8,128)S(1)}) custom-call(bf16[256,512]{1,0:T(8,128)(2,1)S(1)} %copy-done.1, bf16[64,3328]{1,0:T(8,128)(2,1)S(1)} %copy-done, bf16[512,3328]{1,0:T(8,128)(2,1)} %w.1, bf16[256,512]{1,0:T(8,128)(2,1)S(1)} %copy-done.2, f32[8,3328]{1,0:T(8,128)S(1)} %copy-done.3, ...), custom_call_target="tpu_custom_call" | custom-call | tf_op jit(solution)/shard_map/pallas_call | solution.py:364
  130.2 1.8 %copy.12 = bf16[512,3328]{1,0:T(8,128)(2,1)} copy(bf16[512,3328]{1,0:T(8,128)(2,1)S(1)} %get-tuple-element.6) | data formatting | bytes 6815744
  132.0 0.6 copy.13
  132.6 0.6 copy.14
Async XLA Ops:
  0.6 1.0 copy-start
  1.6 0.9 copy-start.1
  2.6 0.9 copy-start.2
  3.5 0.9 copy-start.3
  4.4 0.9 copy-start.4

commit v2 on v0

v2 whole, which is shorter than its diff:
```python
import jax
import jax.numpy as jnp
from jax import lax
from jax.experimental import pallas as pl
from jax.experimental.pallas import tpu as pltpu
from jax.sharding import PartitionSpec as P

STEP = 10
MESH = pl.DeviceIdType.MESH
BF = jnp.bfloat16
F32 = jnp.float32

NZ, NX, NY = 8, 4, 4
NT = 26
NCH = 7
NU = 4

ORDER = [
    ("a_over_x", 3, 1), ("a_over_x", 1, 0), ("q_part",), ("a_start", 0, 0), ("a_start", 0, 1), ("x_send", 2),
    ("x_send", 1), ("a_relay", 1), ("a_relay", 3), ("z_hop", 0, 2), ("x_send", 3), ("a_start", 3, 0),
    ("a_over_x", 3, 0), ("z_hop", 0, 1), ("a_start", 2, 1), ("z_hop", 1, 2), ("x_send", 0), ("a_start", 2, 0),
    ("a_over_x", 1, 1), ("a_start", 1, 0), ("z_hop", 1, 1), ("z_hop", 2, 2), ("a_arrive", 2, 0), ("a_arrive", 2, 1),
    ("a_start", 3, 1), ("a_start", 1, 1), ("z_hop", 2, 1), ("z_hop", 3, 2), ("q_over_z",), ("a_arrive", 3, 0),
    ("m_send",), ("z_hop", 0, 0), ("a_far", 2), ("a_arrive", 1, 0), ("z_hop", 3, 1), ("z_hop", 0, 3),
    ("a_arrive", 3, 1), ("a_done", 2), ("z_hop", 4, 2), ("grad", 2, 2), ("a_arrive", 0, 0), ("a_arrive", 1, 1),
    ("q_over_x",), ("z_hop", 1, 0), ("z_hop", 4, 1), ("a_far", 3), ("grad", 2, 1), ("z_hop", 1, 3), ("a_done", 3),
    ("z_hop", 2, 0), ("a_far", 1), ("grad", 3, 1), ("a_done", 1), ("grad", 1, 1), ("grad", 1, 2), ("a_arrive", 0, 1),
    ("z_hop", 3, 0), ("z_hop", 2, 3), ("grad", 3, 2), ("m_done",), ("q_done",), ("sums", 1), ("z_hop", 4, 0),
    ("grad", 1, 0), ("z_hop", 3, 3), ("grad", 3, 0), ("sums", 0), ("sums", 2), ("z_hop", 4, 3), ("sums", 3),
    ("a_far", 0), ("scale", 1), ("grad", 3, 3), ("grad", 1, 3), ("scale", 2), ("a_done", 0), ("grad", 0, 2),
    ("scale", 0), ("grad", 2, 0), ("update", 3, 1), ("scale", 3), ("grad", 0, 3), ("grad", 2, 3), ("update", 0, 2),
    ("new_moments",), ("grad", 0, 0), ("update", 1, 2), ("update", 2, 2), ("update", 2, 1), ("update", 1, 1),
    ("update", 3, 2), ("grad", 0, 1), ("update", 1, 3), ("update", 0, 1), ("update", 3, 0), ("update", 2, 0),
    ("update", 1, 0), ("update", 0, 3), ("update", 3, 3), ("update", 0, 0), ("update", 2, 3),
]


def kernel(
    act, og, w, pj, m1, m2, ow, o1, o2,
    avm, ogv, pv, wv, m1v, m2v, at, qa, g, gs, gx, prv, pst, mw, s2s, s2r, scs, scr, qpart, qx, qs, qz,
    loc, r_x, r_z, r_g, r_pr, r_s2, r_sc, r_a, r_ax, r_m, r_q,
    snd_x, snd_z, snd_g, snd_pr, snd_s2, snd_sc, snd_a, snd_ax, snd_m, snd_q, outs,
):
    row, col = lax.axis_index("row"), lax.axis_index("col")
    z, x = row // 4, lax.rem(row, 4)
    y, core = col // 2, lax.rem(col, 2)

    def at_z(d):
        return (lax.rem(z + d, NZ) * 4 + x, col)

    def at_x(d):
        return (z * 4 + lax.rem(x + d, NX), col)

    def at_y(d):
        return (row, lax.rem(y + d, NY) * 2 + core)

    def at_col(d):
        return (row, lax.rem(col + d, 8))

    up, down = at_z(1), at_z(NZ - 1)
    y_up, y_down = at_y(1), at_y(NY - 1)
    sibling = (row, y * 2 + 1 - core)

    def tile_start(xx):
        late = jnp.maximum(xx - 2, 0)
        return jnp.where(core == 0, 7 * xx - late, 6 * xx + late)

    def tile_count(xx):
        return jnp.where((xx < 2) == (core == 0), 7, 6)

    def window_start(xx):
        return jnp.minimum(tile_start(xx), NT - NCH)

    def x_of(d):
        return lax.rem(x + d, NX)

    def zrel(d):
        return lax.rem(z + d, NZ)

    start, count = tile_start(x), tile_count(x)

    def send(src, dst, ssem, rsem, target):
        pltpu.make_async_remote_copy(
            src_ref=src, dst_ref=dst, send_sem=ssem, recv_sem=rsem, device_id=target, device_id_type=MESH
        ).start()

    def wait(ref, sem):
        pltpu.make_async_copy(ref, ref, sem).wait()

    def tile(t, n=1):
        return pl.ds(pl.multiple_of(t * 128, 128), n * 128)

    def zblock(zz, begin=0, size=256):
        return pl.ds(pl.multiple_of(zz * 256 + begin, 64), size)

    barrier = pltpu.get_barrier_semaphore()
    partners = [at_z(d) for d in range(1, NZ)] + [at_x(d) for d in range(1, NX)] + [at_col(d) for d in range(1, 8)]
    for partner in partners:
        pl.semaphore_signal(barrier, inc=1, device_id=partner, device_id_type=MESH)

    loads = [(og, ogv), (act, avm), (pj, pv), (m1, m1v), (m2, m2v), (w, wv)]
    for k, (src, dst) in enumerate(loads):
        pltpu.make_async_copy(src, dst, loc.at[k]).start()

    def loaded(k):
        pltpu.make_async_copy(*loads[k], loc.at[k]).wait()

    own_lanes = pl.ds(pl.multiple_of(col * 256, 256), 256)

    def panel_rows(xx, begin=0, size=512):
        return pl.ds(pl.multiple_of(xx * 512 + begin, 256), size)

    def first_tile(u):
        return max(2 * u - 1, 0)

    def with_width(u, tiles, f):
        if u < NU - 1:
            f(1 if u == 0 else 2)
        else:
            pl.when(tiles == NCH)(lambda: f(2))
            pl.when(tiles == NCH - 1)(lambda: f(1))

    def low(n):
        return pl.ds(0, 128 * n)

    loaded(1)
    at[panel_rows(x), own_lanes] = avm[...].T
    loaded(0)
    g_rows = zblock(z, 64 * x, 64)
    for u in range(NU):

        def keep(n, u=u):
            g[u, g_rows, low(n)] = ogv[:, tile(start + first_tile(u), n)]
            if n == 1:
                g[u, :, pl.ds(128, 128)] = jnp.zeros((2048, 128), BF)

        with_width(u, count, keep)
    mw[:, :, :, pl.ds(NCH * 128, 128)] = jnp.zeros((4, 2, 8, 128), F32)
    pl.semaphore_wait(barrier, len(partners))

    def x_send(u):
        for d in (2, 1, 3):
            xx = x_of(d)

            def go(n, d=d, xx=xx):
                mine = ogv.at[:, tile(tile_start(xx) + first_tile(u), n)]
                send(mine, g.at[u, g_rows, low(n)], snd_x.at[d - 1, u], r_x.at[u], at_x(d))

            with_width(u, tile_count(xx), go)

    def z_hop(hop, u):
        lower, upper = zrel(NZ - hop), zrel(hop)

        def go(n):
            def move(zz, a, b, sem, target):
                part = g.at[u, zblock(zz, a, b), low(n)]
                send(part, part, snd_z.at[u], r_z.at[u, sem], target)

            def arrive(zz, sem):
                wait(g.at[u, zblock(zz), low(n)], r_z.at[u, sem])

            if hop == 0:
                wait(g.at[u, pl.ds(0, 192), low(n)], r_x.at[u])
                move(z, 0, 256, 0, up)
                move(z, 0, 256, 1, down)
            elif hop == 4:
                arrive(lower, 6)
            else:
                last = hop == 3
                arrive(lower, 2 * hop - 2)
                move(lower, 0, 128 if last else 256, 6 if last else 2 * hop, up)
                arrive(upper, 2 * hop - 1)
                move(upper, 128 if last else 0, 128 if last else 256, 6 if last else 2 * hop + 1, down)

        with_width(u, count, go)

    def a_ref(d, yy, begin, size):
        lanes = pl.ds(pl.multiple_of((yy * 2 + core) * 256, 256), 256)
        return at.at[panel_rows(x_of(d), begin, size), lanes]

    def a_send(d, yy, begin, size, sem, target):
        part = a_ref(d, yy, begin, size)
        send(part, part, snd_a.at[d], r_a.at[d, sem], target)

    def a_over_x(d, h):
        part = at.at[panel_rows(x, 256 * h, 256), own_lanes]
        send(part, part, snd_ax, r_ax.at[NX - d, h], at_x(d))

    over_x_seen = set()

    def over_x(d, h):
        if (d, h) not in over_x_seen:
            over_x_seen.add((d, h))
            wait(a_ref(d, y, 256 * h, 256), r_ax.at[d, h])

    def a_relay(d):
        h = 0 if d == 3 else 1
        over_x(d, h)
        part = a_ref(d, y, 256 * h, 256)
        send(part, part, snd_ax, r_ax.at[2, h], at_x(NX - d))

    def a_start(d, h):
        if d:
            over_x(d, h)
        a_send(d, y, 256 * h, 256, h, y_up)
        a_send(d, y, 256 * h, 256, 2 + h, y_down)
        a_send(d, y, 256 * h, 256, 6, sibling)

    y_lower, y_upper, y_far = lax.rem(y + 3, NY), lax.rem(y + 1, NY), lax.rem(y + 2, NY)

    def a_arrive(d, h):
        wait(a_ref(d, y_lower, 256 * h, 256), r_a.at[d, h])
        if h == 0:
            a_send(d, y_lower, 0, 256, 4, y_up)
        wait(a_ref(d, y_upper, 256 * h, 256), r_a.at[d, 2 + h])
        if h == 1:
            a_send(d, y_upper, 256, 256, 5, y_down)
        a_send(d, y_lower, 256 * h, 256, 6, sibling)
        a_send(d, y_upper, 256 * h, 256, 6, sibling)

    def a_far(d):
        wait(a_ref(d, y_far, 0, 256), r_a.at[d, 4])
        wait(a_ref(d, y_far, 256, 256), r_a.at[d, 5])
        a_send(d, y_far, 0, 512, 6, sibling)

    def a_done(d):
        wait(at.at[pl.ds(0, 512), pl.ds(0, 1024)], r_a.at[d, 6])

    def q_part():
        loaded(2)
        q = lax.dot_general(pv[...], avm[...], (((1,), (1,)), ((), ())), preferred_element_type=F32)
        for zz in range(NZ):
            qpart[zz] = q[32 * zz : 32 * zz + 32]
        for d in range(1, NZ):
            send(qpart.at[zrel(d)], qz.at[d - 1], snd_q.at[0], r_q.at[0], at_z(d))

    def q_over_z():
        wait(qz, r_q.at[0])
        q = qpart[z]
        for d in range(NZ - 1):
            q = q + qz[d]
        qs[...] = q
        for d in (2, 1, 3):
            send(qs, qx.at[d - 1], snd_q.at[1], r_q.at[1], at_x(d))

    def q_over_x():
        wait(qx, r_q.at[1])
        q = qs[...] + qx[0] + qx[1] + qx[2]
        high = q.astype(BF).astype(F32)
        rest = q - high
        parts = []
        for xx in range(NX):
            parts += [high[8 * xx : 8 * xx + 8], rest[8 * xx : 8 * xx + 8]]
        qa[:, own_lanes] = jnp.concatenate(parts, axis=0).astype(BF)
        part = qa.at[:, own_lanes]
        for d in range(1, 8):
            send(part, part, snd_q.at[2], r_q.at[2], at_col(d))

    def q_done():
        wait(qa.at[:, pl.ds(0, 1792)], r_q.at[2])

    def m_send():
        loaded(3)
        loaded(4)
        own = tile(window_start(x), NCH)
        mw[x, 0, :, low(NCH)] = m1v[:, own]
        mw[x, 1, :, low(NCH)] = m2v[:, own]
        for d in range(1, NX):
            cols = tile(window_start(x_of(d)), NCH)
            send(m1v.at[:, cols], mw.at[x, 0, :, low(NCH)], snd_m, r_m, at_x(d))
            send(m2v.at[:, cols], mw.at[x, 1, :, low(NCH)], snd_m, r_m, at_x(d))

    def m_done():
        wait(mw.at[pl.ds(0, 3), :, :, low(NCH)], r_m)

    def grad(d, u):
        total = jnp.dot(at[panel_rows(x_of(d)), :], g[u], preferred_element_type=F32).astype(BF)
        if d:
            gs[d - 1, u] = total

        def go(n):
            cols = tile(start + first_tile(u), n)
            if d:
                send(gs.at[d - 1, u, :, low(n)], gx.at[:, cols], snd_g.at[u], r_g.at[NX - d - 1, u], at_x(d))
            else:
                gx[:, cols] = total[:, : 128 * n]

        with_width(u, count, go)

    def moments(first_moment, second_moment, proj):
        first = 0.9 * first_moment + 0.1 * proj
        second = 0.999 * second_moment + 0.001 * proj * proj
        return first, second

    def sums(u):
        total = jnp.dot(qa[...], g[u], preferred_element_type=F32)
        lanes = tile(start - window_start(x) + first_tile(u), 2)
        normed_sq = jnp.zeros((8, 256), F32)
        proj_sq = jnp.zeros((8, 256), F32)
        wide = 1 if u == 0 else 2
        for xx in range(NX):
            proj = total[16 * xx : 16 * xx + 8] + total[16 * xx + 8 : 16 * xx + 16]
            pst[xx, :, tile(first_tile(u), wide)] = proj[:, : 128 * wide]
            first, second = moments(mw[xx, 0, :, lanes], mw[xx, 1, :, lanes], proj)
            normed = first / (1.0 - 0.9**STEP) / (jnp.sqrt(second / (1.0 - 0.999**STEP)) + 1e-08)
            normed_sq = normed_sq + normed * normed
            proj_sq = proj_sq + proj * proj
        normed_sq = jnp.sum(normed_sq, axis=0, keepdims=True)
        proj_sq = jnp.sum(proj_sq, axis=0, keepdims=True)
        s2s[u, 0:1] = normed_sq[:, :128]
        s2s[u, 1:2] = proj_sq[:, :128]
        s2s[u, 2:3] = normed_sq[:, 128:]
        s2s[u, 3:4] = proj_sq[:, 128:]
        s2s[u, 4:8] = jnp.zeros((4, 128), F32)
        for d in range(1, NZ):
            send(s2s.at[u], s2r.at[u, d - 1], snd_s2.at[u], r_s2.at[u], at_z(d))
        if u == NU - 1:
            for tiles in (NCH - 1, NCH):

                @pl.when(count == tiles)
                def _(tiles=tiles):
                    cols = tile(start, tiles)
                    prv[:, cols] = pst[x, :, low(tiles)]
                    for d in (2, 1, 3):
                        send(pst.at[x_of(d), :, low(tiles)], prv.at[:, cols], snd_pr, r_pr.at[NX - d - 1], at_x(d))

    def scale(u):
        wait(s2r.at[u], r_s2.at[u])
        total = s2s[u]
        for d in range(NZ - 1):
            total = total + s2r[u, d]
        left = jnp.sqrt(total[0:1]) / jnp.sqrt(total[1:2] + 1e-06)
        right = jnp.sqrt(total[2:3]) / jnp.sqrt(total[3:4] + 1e-06)
        scs[u] = jnp.broadcast_to(jnp.concatenate([left, right], axis=1), (8, 256))

        def go(n):
            cols = tile(start + first_tile(u), n)
            scr[:, cols] = scs[u, :, low(n)]
            for d in (2, 1, 3):
                send(scs.at[u, :, low(n)], scr.at[:, cols], snd_sc.at[u], r_sc.at[NX - d - 1, u], at_x(d))

        with_width(u, count, go)

    weights_seen = []

    def update(d, u):
        back = (NX - d) % NX
        xx = x_of(back)
        if not weights_seen:
            weights_seen.append(True)
            loaded(5)

        def go(n):
            cols = tile(tile_start(xx) + first_tile(u), n)
            if d:
                wait(scr.at[:, cols], r_sc.at[back - 1, u])
                wait(gx.at[:, cols], r_g.at[back - 1, u])
            step = 0.01 * scr[0:1, cols]
            wv[:, cols] = (wv[:, cols].astype(F32) - step * gx[:, cols].astype(F32)).astype(BF)
            pltpu.make_async_copy(wv.at[:, cols], ow.at[:, cols], outs.at[0]).start()

        with_width(u, tile_count(xx), go)

    def new_moments():
        for d in range(1, NX):
            xx = x_of(d)
            for tiles in (NCH - 1, NCH):

                @pl.when(tile_count(xx) == tiles)
                def _(tiles=tiles):
                    wait(prv.at[:, tile(tile_start(xx), tiles)], r_pr.at[d - 1])

        wait(mw.at[pl.ds(0, 3), :, :, low(NCH)], snd_m)
        m1v[...], m2v[...] = moments(m1v[...], m2v[...], prv[...])
        pltpu.make_async_copy(m1v, o1, outs.at[1]).start()
        pltpu.make_async_copy(m2v, o2, outs.at[2]).start()

    steps = dict(
        x_send=x_send, z_hop=z_hop, a_over_x=a_over_x, a_relay=a_relay, a_start=a_start, a_arrive=a_arrive,
        a_far=a_far, a_done=a_done, q_part=q_part, q_over_z=q_over_z, q_over_x=q_over_x, q_done=q_done,
        m_send=m_send, m_done=m_done, grad=grad, sums=sums, scale=scale, update=update, new_moments=new_moments,
    )
    for name, *numbers in ORDER:
        steps[name](*numbers)

    for u in range(NU):

        def drain(n, u=u):
            wait(g.at[u, pl.ds(0, 1792), low(n)], snd_z.at[u])
            wait(gs.at[:, u, :, low(n)], snd_g.at[u])
            wait(scr.at[:, low(3 * n)], snd_sc.at[u])

        with_width(u, count, drain)
        wait(s2r.at[u], snd_s2.at[u])
        for d in range(1, NX):
            with_width(u, tile_count(x_of(d)), lambda n, u=u, d=d: wait(ogv.at[:, low(n)], snd_x.at[d - 1, u]))
    for tiles in (NCH - 1, NCH):
        pl.when(count == tiles)(lambda tiles=tiles: wait(pst.at[pl.ds(0, 3), :, low(tiles)], snd_pr))
    for d in range(NX):
        wait(at.at[pl.ds(0, 512), pl.ds(0, 1792)], snd_a.at[d])
    wait(at.at[pl.ds(0, 512), pl.ds(0, 768)], snd_ax)
    wait(qz, snd_q.at[0])
    wait(qx, snd_q.at[1])
    wait(qa.at[:, pl.ds(0, 1792)], snd_q.at[2])
    wait(m1v, outs.at[1])
    wait(m2v, outs.at[2])
    wait(wv, outs.at[0])


def shards(activations, out_grads, weights, projector, first_moment, second_moment):
    vm, dma = pltpu.VMEM, pltpu.SemaphoreType.DMA
    operands = (activations, out_grads, weights, projector, first_moment, second_moment)
    operands = [pltpu.with_memory_space_constraint(operand, pltpu.HBM) for operand in operands]
    return pl.pallas_call(
        kernel,
        out_shape=(
            jax.ShapeDtypeStruct((512, 3328), BF),
            jax.ShapeDtypeStruct((8, 3328), F32),
            jax.ShapeDtypeStruct((8, 3328), F32),
        ),
        in_specs=[pl.BlockSpec(memory_space=pl.ANY)] * 6,
        out_specs=(pl.BlockSpec(memory_space=pl.ANY),) * 3,
        scratch_shapes=[
            vm((256, 512), BF),
            vm((64, 3328), BF),
            vm((256, 512), BF),
            vm((512, 3328), BF),
            vm((8, 3328), F32),
            vm((8, 3328), F32),
            vm((2048, 2048), BF),
            vm((64, 2048), BF),
            vm((NU, 2048, 256), BF),
            vm((3, NU, 512, 256), BF),
            vm((512, 3328), BF),
            vm((8, 3328), F32),
            vm((4, 8, 1024), F32),
            vm((4, 2, 8, 1024), F32),
            vm((NU, 8, 128), F32),
            vm((NU, 7, 8, 128), F32),
            vm((NU, 8, 256), F32),
            vm((8, 3328), F32),
            vm((8, 32, 256), F32),
            vm((3, 32, 256), F32),
            vm((32, 256), F32),
            vm((7, 32, 256), F32),
            dma((6,)),
            dma((NU,)),
            dma((NU, 7)),
            dma((3, NU)),
            dma((3,)),
            dma((NU,)),
            dma((3, NU)),
            dma((NX, 7)),
            dma((NX, 2)),
            dma,
            dma((3,)),
            dma((3, NU)),
            dma((NU,)),
            dma((NU,)),
            dma,
            dma((NU,)),
            dma((NU,)),
            dma((NX,)),
            dma,
            dma,
            dma((3,)),
            dma((3,)),
        ],
        compiler_params=pltpu.CompilerParams(
            collective_id=0, has_side_effects=True, vmem_limit_bytes=48 * 1024 * 1024
        ),
    )(*operands)


def solution(mesh):
    return jax.shard_map(
        shards,
        mesh=mesh,
        in_specs=(
            P("col", "row"),
            P("row", "col"),
            P("row", "col"),
            P(None, "row"),
            P("row", "col"),
            P("row", "col"),
        ),
        out_specs=(P("row", "col"), P("row", "col"), P("row", "col")),
        check_vma=False,
    )
```

time: 500 us -> 87.7 us (0.18)
  the two profiles are of different devices: /device:TPU:8 before, /device:TPU:1 now
where the time goes in v2:
time: 87.7 us; the launch traced here: 87.6 us
  Pallas kernels  84 us (96%)
  local copies, waits for them, and re-layouts  3.04 us (3%)
    pallas_call x1, Pallas kernels, shards(): pl.pallas_call(kernel, out_shape=(jax.ShapeDtypeStruct((512, 3328), BF),...  84 us
    unnamed x3, local copies, waits for them, and re-layouts  3.04 us

profile of v2, /device:TPU:1, one launch (start us, length us, event | category | flops | bytes accessed | tf_op | source)
XLA Modules:
  0.0 87.6 jit_solution(14207994877510408481)
XLA Ops:
  0.6 84.0 %shard_map.85 = (bf16[512,3328]{1,0:T(8,128)(2,1)S(1)}, f32[8,3328]{1,0:T(8,128)S(1)}, f32[8,3328]{1,0:T(8,128)S(1)}) custom-call(bf16[256,512]{1,0:T(8,128)(2,1)} %act.1, bf16[64,3328]{1,0:T(8,128)(2,1)} %og.1, bf16[512,3328]{1,0:T(8,128)(2,1)} %w.1, bf16[256,512]{1,0:T(8,128)(2,1)} %pj.1, f32[8,3328]{1,0:T(8,128)} %m1.1, f32[8,3328]{1,0:T(8,128)} %m2.1), custom_call_target="tpu_custom_call" | custom-call | tf_op jit(solution)/shard_map/pallas_call | solution.py:414
  84.6 1.8 %copy.12 = bf16[512,3328]{1,0:T(8,128)(2,1)} copy(bf16[512,3328]{1,0:T(8,128)(2,1)S(1)} %get-tuple-element.6) | data formatting | bytes 6815744
  86.4 0.6 copy.13
  87.0 0.6 copy.14

commit v3 on v2

--- a/solution.py
+++ b/solution.py
@@ -16,27 +16,33 @@
 NU = 4
 
 ORDER = [
-    ("a_over_x", 3, 1), ("a_over_x", 1, 0), ("q_part",), ("a_start", 0, 0), ("a_start", 0, 1), ("x_send", 2),
-    ("x_send", 1), ("a_relay", 1), ("a_relay", 3), ("z_hop", 0, 2), ("x_send", 3), ("a_start", 3, 0),
-    ("a_over_x", 3, 0), ("z_hop", 0, 1), ("a_start", 2, 1), ("z_hop", 1, 2), ("x_send", 0), ("a_start", 2, 0),
-    ("a_over_x", 1, 1), ("a_start", 1, 0), ("z_hop", 1, 1), ("z_hop", 2, 2), ("a_arrive", 2, 0), ("a_arrive", 2, 1),
-    ("a_start", 3, 1), ("a_start", 1, 1), ("z_hop", 2, 1), ("z_hop", 3, 2), ("q_over_z",), ("a_arrive", 3, 0),
-    ("m_send",), ("z_hop", 0, 0), ("a_far", 2), ("a_arrive", 1, 0), ("z_hop", 3, 1), ("z_hop", 0, 3),
-    ("a_arrive", 3, 1), ("a_done", 2), ("z_hop", 4, 2), ("grad", 2, 2), ("a_arrive", 0, 0), ("a_arrive", 1, 1),
-    ("q_over_x",), ("z_hop", 1, 0), ("z_hop", 4, 1), ("a_far", 3), ("grad", 2, 1), ("z_hop", 1, 3), ("a_done", 3),
-    ("z_hop", 2, 0), ("a_far", 1), ("grad", 3, 1), ("a_done", 1), ("grad", 1, 1), ("grad", 1, 2), ("a_arrive", 0, 1),
-    ("z_hop", 3, 0), ("z_hop", 2, 3), ("grad", 3, 2), ("m_done",), ("q_done",), ("sums", 1), ("z_hop", 4, 0),
-    ("grad", 1, 0), ("z_hop", 3, 3), ("grad", 3, 0), ("sums", 0), ("sums", 2), ("z_hop", 4, 3), ("sums", 3),
-    ("a_far", 0), ("scale", 1), ("grad", 3, 3), ("grad", 1, 3), ("scale", 2), ("a_done", 0), ("grad", 0, 2),
-    ("scale", 0), ("grad", 2, 0), ("update", 3, 1), ("scale", 3), ("grad", 0, 3), ("grad", 2, 3), ("update", 0, 2),
-    ("new_moments",), ("grad", 0, 0), ("update", 1, 2), ("update", 2, 2), ("update", 2, 1), ("update", 1, 1),
-    ("update", 3, 2), ("grad", 0, 1), ("update", 1, 3), ("update", 0, 1), ("update", 3, 0), ("update", 2, 0),
-    ("update", 1, 0), ("update", 0, 3), ("update", 3, 3), ("update", 0, 0), ("update", 2, 3),
+    ("a_over_x", 3, 1), ("q_part",), ("x_send", 2), ("a_over_x", 1, 0), ("x_send", 1), ("a_start", 1, 1),
+    ("a_over_x", 3, 0), ("z_hop", 0, 2), ("x_send", 0), ("a_start", 3, 0), ("a_over_x", 1, 1), ("z_hop", 0, 1),
+    ("a_relay", 3), ("a_start", 1, 0), ("z_hop", 1, 2), ("a_start", 3, 1), ("z_hop", 1, 1), ("a_relay", 1),
+    ("a_arrive", 3, 0), ("q_over_z",), ("a_arrive", 1, 1), ("a_arrive", 1, 0), ("z_hop", 2, 2), ("x_send", 3),
+    ("a_arrive", 3, 1), ("a_start", 2, 0), ("z_hop", 2, 1), ("z_hop", 3, 2), ("m_send",), ("z_hop", 0, 0),
+    ("a_far", 1), ("a_start", 2, 1), ("a_far", 3), ("z_hop", 3, 1), ("z_hop", 0, 3), ("a_done", 3), ("q_over_x",),
+    ("a_done", 1), ("z_hop", 4, 2), ("grad", 1, 2), ("grad", 3, 2), ("a_arrive", 2, 0), ("z_hop", 1, 0),
+    ("a_arrive", 2, 1), ("a_start", 0, 0), ("z_hop", 4, 1), ("m_done",), ("grad", 3, 1), ("z_hop", 1, 3),
+    ("grad", 1, 1), ("q_done",), ("z_hop", 2, 0), ("a_start", 0, 1), ("sums", 1), ("a_far", 2), ("sums", 2),
+    ("z_hop", 2, 3), ("a_done", 2), ("grad", 2, 2), ("z_hop", 3, 0), ("a_arrive", 0, 1), ("z_hop", 3, 3),
+    ("z_hop", 4, 0), ("scale", 2), ("grad", 2, 0), ("scale", 1), ("sums", 0), ("a_arrive", 0, 0), ("z_hop", 4, 3),
+    ("sums", 3), ("grad", 2, 3), ("grad", 3, 3), ("grad", 1, 3), ("update", 1, 2), ("a_far", 0), ("scale", 0),
+    ("grad", 1, 0), ("update", 3, 1), ("a_done", 0), ("scale", 3), ("grad", 0, 1), ("proj_out",), ("grad", 0, 2),
+    ("grad", 2, 1), ("grad", 0, 0), ("grad", 0, 3), ("update", 0, 2), ("grad", 3, 0), ("update", 1, 3),
+    ("update", 1, 0), ("update", 2, 3), ("update", 0, 3), ("update", 1, 1), ("update", 3, 3), ("update", 3, 2),
+    ("update", 0, 0), ("update", 0, 1), ("update", 2, 2), ("update", 2, 0), ("update", 2, 1), ("update", 3, 0),
 ]
 
 
+def moments(first_moment, second_moment, proj):
+    first = 0.9 * first_moment + 0.1 * proj
+    second = 0.999 * second_moment + 0.001 * proj * proj
+    return first, second
+
+
 def kernel(
-    act, og, w, pj, m1, m2, ow, o1, o2,
+    act, og, w, pj, m1, m2, ow, o1,
     avm, ogv, pv, wv, m1v, m2v, at, qa, g, gs, gx, prv, pst, mw, s2s, s2r, scs, scr, qpart, qx, qs, qz,
     loc, r_x, r_z, r_g, r_pr, r_s2, r_sc, r_a, r_ax, r_m, r_q,
     snd_x, snd_z, snd_g, snd_pr, snd_s2, snd_sc, snd_a, snd_ax, snd_m, snd_q, outs,
@@ -286,11 +292,6 @@
                 gx[:, cols] = total[:, : 128 * n]
 
         with_width(u, count, go)
-
-    def moments(first_moment, second_moment, proj):
-        first = 0.9 * first_moment + 0.1 * proj
-        second = 0.999 * second_moment + 0.001 * proj * proj
-        return first, second
 
     def sums(u):
         total = jnp.dot(qa[...], g[u], preferred_element_type=F32)
@@ -361,7 +362,7 @@
 
         with_width(u, tile_count(xx), go)
 
-    def new_moments():
+    def proj_out():
         for d in range(1, NX):
             xx = x_of(d)
             for tiles in (NCH - 1, NCH):
@@ -370,15 +371,12 @@
                 def _(tiles=tiles):
                     wait(prv.at[:, tile(tile_start(xx), tiles)], r_pr.at[d - 1])
 
-        wait(mw.at[pl.ds(0, 3), :, :, low(NCH)], snd_m)
-        m1v[...], m2v[...] = moments(m1v[...], m2v[...], prv[...])
-        pltpu.make_async_copy(m1v, o1, outs.at[1]).start()
-        pltpu.make_async_copy(m2v, o2, outs.at[2]).start()
+        pltpu.make_async_copy(prv, o1, outs.at[1]).start()
 
     steps = dict(
         x_send=x_send, z_hop=z_hop, a_over_x=a_over_x, a_relay=a_relay, a_start=a_start, a_arrive=a_arrive,
         a_far=a_far, a_done=a_done, q_part=q_part, q_over_z=q_over_z, q_over_x=q_over_x, q_done=q_done,
-        m_send=m_send, m_done=m_done, grad=grad, sums=sums, scale=scale, update=update, new_moments=new_moments,
+        m_send=m_send, m_done=m_done, grad=grad, sums=sums, scale=scale, update=update, proj_out=proj_out,
     )
     for name, *numbers in ORDER:
         steps[name](*numbers)
@@ -402,8 +400,8 @@
     wait(qz, snd_q.at[0])
     wait(qx, snd_q.at[1])
     wait(qa.at[:, pl.ds(0, 1792)], snd_q.at[2])
-    wait(m1v, outs.at[1])
-    wait(m2v, outs.at[2])
+    wait(mw.at[pl.ds(0, 3), :, :, low(NCH)], snd_m)
+    wait(prv, outs.at[1])
     wait(wv, outs.at[0])
 
 
@@ -411,15 +409,14 @@
     vm, dma = pltpu.VMEM, pltpu.SemaphoreType.DMA
     operands = (activations, out_grads, weights, projector, first_moment, second_moment)
     operands = [pltpu.with_memory_space_constraint(operand, pltpu.HBM) for operand in operands]
-    return pl.pallas_call(
+    new_weights, proj = pl.pallas_call(
         kernel,
         out_shape=(
             jax.ShapeDtypeStruct((512, 3328), BF),
             jax.ShapeDtypeStruct((8, 3328), F32),
-            jax.ShapeDtypeStruct((8, 3328), F32),
         ),
         in_specs=[pl.BlockSpec(memory_space=pl.ANY)] * 6,
-        out_specs=(pl.BlockSpec(memory_space=pl.ANY),) * 3,
+        out_specs=(pl.BlockSpec(memory_space=pl.ANY),) * 2,
         scratch_shapes=[
             vm((256, 512), BF),
             vm((64, 3328), BF),
@@ -464,12 +461,13 @@
             dma,
             dma,
             dma((3,)),
-            dma((3,)),
+            dma((2,)),
         ],
         compiler_params=pltpu.CompilerParams(
             collective_id=0, has_side_effects=True, vmem_limit_bytes=48 * 1024 * 1024
         ),
     )(*operands)
+    return (new_weights, *moments(first_moment, second_moment, proj))
 
 
 def solution(mesh):

time: 87.7 us -> 85.4 us (0.974)
  Pallas kernels: 84 us -> 82.2 us
  local copies, waits for them, and re-layouts: 3.04 us -> 1.76 us
    pallas_call x1, Pallas kernels: 84 us -> 82.2 us  [shards(): pl.pallas_call(kernel, out_shape=(jax.ShapeDtypeStruct((512, 3328), BF),...]
    unnamed x3 -> x5, local copies, waits for them, and re-layouts: 3.04 us -> 1.76 us
where the time goes in v3:
time: 85.4 us; the launch traced here: 85.3 us
  Pallas kernels  82.2 us (96%)
  local copies, waits for them, and re-layouts  1.76 us (2%)
    pallas_call x1, Pallas kernels, shards(): pl.pallas_call(kernel, out_shape=(jax.ShapeDtypeStruct((512, 3328), BF),...  82.2 us
    unnamed x5, local copies, waits for them, and re-layouts  1.76 us

profile of v3, /device:TPU:1, one launch (start us, length us, event | category | flops | bytes accessed | tf_op | source)
XLA Modules:
  0.0 85.3 jit_solution(14391964743275250577)
XLA Ops:
  0.6 0.0 copy-start.1
  0.6 0.0 copy-start
  0.7 82.2 %shard_map.85 = (bf16[512,3328]{1,0:T(8,128)(2,1)S(1)}, f32[8,3328]{1,0:T(8,128)S(1)}) custom-call(bf16[256,512]{1,0:T(8,128)(2,1)} %act.1, bf16[64,3328]{1,0:T(8,128)(2,1)} %og.1, bf16[512,3328]{1,0:T(8,128)(2,1)} %w.1, bf16[256,512]{1,0:T(8,128)(2,1)} %pj.1, f32[8,3328]{1,0:T(8,128)} %m1.1, f32[8,3328]{1,0:T(8,128)} %m2.1), custom_call_target="tpu_custom_call" | custom-call | tf_op jit(solution)/shard_map/pallas_call | solution.py:412
  82.8 0.0 copy-done.1
  82.8 0.0 copy-done
  82.8 0.7 fusion
  83.6 1.8 %copy.10 = bf16[512,3328]{1,0:T(8,128)(2,1)} copy(bf16[512,3328]{1,0:T(8,128)(2,1)S(1)} %get-tuple-element.12) | data formatting | bytes 6815744
Async XLA Ops:
  0.6 82.2 %copy-start.1 = (f32[8,3328]{1,0:T(8,128)S(1)}, f32[8,3328]{1,0:T(8,128)}, u32[]{:S(2)}) copy-start(f32[8,3328]{1,0:T(8,128)} %m2.1) | copy-start | bytes 319492
  0.6 82.2 %copy-start = (f32[8,3328]{1,0:T(8,128)S(1)}, f32[8,3328]{1,0:T(8,128)}, u32[]{:S(2)}) copy-start(f32[8,3328]{1,0:T(8,128)} %m1.1) | copy-start | bytes 319492

commit v4 on v3

--- a/solution.py
+++ b/solution.py
@@ -373,34 +373,38 @@
 
         pltpu.make_async_copy(prv, o1, outs.at[1]).start()
 
+    def sends_done():
+        for u in range(NU):
+
+            def drain(n, u=u):
+                wait(g.at[u, pl.ds(0, 1792), low(n)], snd_z.at[u])
+                wait(gs.at[:, u, :, low(n)], snd_g.at[u])
+                wait(scr.at[:, low(3 * n)], snd_sc.at[u])
+
+            with_width(u, count, drain)
+            wait(s2r.at[u], snd_s2.at[u])
+            for d in range(1, NX):
+                with_width(u, tile_count(x_of(d)), lambda n, u=u, d=d: wait(ogv.at[:, low(n)], snd_x.at[d - 1, u]))
+        for tiles in (NCH - 1, NCH):
+            pl.when(count == tiles)(lambda tiles=tiles: wait(pst.at[pl.ds(0, 3), :, low(tiles)], snd_pr))
+        for d in range(NX):
+            wait(at.at[pl.ds(0, 512), pl.ds(0, 1792)], snd_a.at[d])
+        wait(at.at[pl.ds(0, 512), pl.ds(0, 768)], snd_ax)
+        wait(qz, snd_q.at[0])
+        wait(qx, snd_q.at[1])
+        wait(qa.at[:, pl.ds(0, 1792)], snd_q.at[2])
+        wait(mw.at[pl.ds(0, 3), :, :, low(NCH)], snd_m)
+
     steps = dict(
         x_send=x_send, z_hop=z_hop, a_over_x=a_over_x, a_relay=a_relay, a_start=a_start, a_arrive=a_arrive,
         a_far=a_far, a_done=a_done, q_part=q_part, q_over_z=q_over_z, q_over_x=q_over_x, q_done=q_done,
         m_send=m_send, m_done=m_done, grad=grad, sums=sums, scale=scale, update=update, proj_out=proj_out,
     )
-    for name, *numbers in ORDER:
+    for position, (name, *numbers) in enumerate(ORDER):
+        if position == len(ORDER) - 2:
+            sends_done()
         steps[name](*numbers)
 
-    for u in range(NU):
-
-        def drain(n, u=u):
-            wait(g.at[u, pl.ds(0, 1792), low(n)], snd_z.at[u])
-            wait(gs.at[:, u, :, low(n)], snd_g.at[u])
-            wait(scr.at[:, low(3 * n)], snd_sc.at[u])
-
-        with_width(u, count, drain)
-        wait(s2r.at[u], snd_s2.at[u])
-        for d in range(1, NX):
-            with_width(u, tile_count(x_of(d)), lambda n, u=u, d=d: wait(ogv.at[:, low(n)], snd_x.at[d - 1, u]))
-    for tiles in (NCH - 1, NCH):
-        pl.when(count == tiles)(lambda tiles=tiles: wait(pst.at[pl.ds(0, 3), :, low(tiles)], snd_pr))
-    for d in range(NX):
-        wait(at.at[pl.ds(0, 512), pl.ds(0, 1792)], snd_a.at[d])
-    wait(at.at[pl.ds(0, 512), pl.ds(0, 768)], snd_ax)
-    wait(qz, snd_q.at[0])
-    wait(qx, snd_q.at[1])
-    wait(qa.at[:, pl.ds(0, 1792)], snd_q.at[2])
-    wait(mw.at[pl.ds(0, 3), :, :, low(NCH)], snd_m)
     wait(prv, outs.at[1])
     wait(wv, outs.at[0])
 

time: 85.4 us -> 85.3 us (level)
  no operation moved by 1% of the time
where the time goes in v4:
time: 85.3 us; the launch traced here: 85.2 us
  Pallas kernels  82.1 us (96%)
  local copies, waits for them, and re-layouts  1.76 us (2%)
    pallas_call x1, Pallas kernels, shards(): pl.pallas_call(kernel, out_shape=(jax.ShapeDtypeStruct((512, 3328), BF),...  82.1 us
    unnamed x5, local copies, waits for them, and re-layouts  1.76 us

profile of v4, /device:TPU:1, one launch (start us, length us, event | category | flops | bytes accessed | tf_op | source)
XLA Modules:
  0.0 85.2 jit_solution(8008138704204739617)
XLA Ops:
  0.6 0.0 copy-start.1
  0.6 0.0 copy-start
  0.7 82.1 %shard_map.85 = (bf16[512,3328]{1,0:T(8,128)(2,1)S(1)}, f32[8,3328]{1,0:T(8,128)S(1)}) custom-call(bf16[256,512]{1,0:T(8,128)(2,1)} %act.1, bf16[64,3328]{1,0:T(8,128)(2,1)} %og.1, bf16[512,3328]{1,0:T(8,128)(2,1)} %w.1, bf16[256,512]{1,0:T(8,128)(2,1)} %pj.1, f32[8,3328]{1,0:T(8,128)} %m1.1, f32[8,3328]{1,0:T(8,128)} %m2.1), custom_call_target="tpu_custom_call" | custom-call | tf_op jit(solution)/shard_map/pallas_call | solution.py:416
  82.8 0.0 copy-done.1
  82.8 0.0 copy-done
  82.8 0.7 fusion
  83.5 1.8 %copy.10 = bf16[512,3328]{1,0:T(8,128)(2,1)} copy(bf16[512,3328]{1,0:T(8,128)(2,1)S(1)} %get-tuple-element.12) | data formatting | bytes 6815744
Async XLA Ops:
  0.6 82.1 %copy-start.1 = (f32[8,3328]{1,0:T(8,128)S(1)}, f32[8,3328]{1,0:T(8,128)}, u32[]{:S(2)}) copy-start(f32[8,3328]{1,0:T(8,128)} %m2.1) | copy-start | bytes 319492
  0.6 82.1 %copy-start = (f32[8,3328]{1,0:T(8,128)S(1)}, f32[8,3328]{1,0:T(8,128)}, u32[]{:S(2)}) copy-start(f32[8,3328]{1,0:T(8,128)} %m1.1) | copy-start | bytes 319492
